TPU v7x, 256 devices: a whole 4x4x8 slice. The times are simulated.
256 devices in a mesh: seq: 32 (over z, y), head: 8 (over x, core).
Axes of the slice: x: 4, y: 4, z: 8, core: 2. Of those that a mesh axis runs over, the one named last changes fastest.
Arguments:
- grad_y: bfloat16 [16384, 4096], P('seq', 'head'), may hold values from -6 to 6
- w_out: bfloat16 [4096, 4096], P('head'), may hold values from -0.09375 to 0.09375
- queries: bfloat16 [16384, 4096], P('seq', 'head'), may hold values from -6 to 6
- keys: bfloat16 [16384, 4096], P('seq', 'head'), may hold values from -6 to 6
- values: bfloat16 [16384, 4096], P('seq', 'head'), may hold values from -6 to 6
- level_rows: int32 [16384], P('seq'), may hold values from 0 to 127
- level_table: float32 [128, 12, 32], P(None, None, 'head'), may hold values from 0.2 to 3
Outputs:
- query_grad: float32 [16384, 4096], P('seq', 'head')
- key_grad: float32 [16384, 4096], P('seq', 'head')
- value_grad: float32 [16384, 4096], P('seq', 'head')
Inputs may be any that keep to these rules, and one draw needn't show every extreme that they name: `level_rows`: each token names one row of the level-weight table.
All inputs are finite; a program needn't handle non-finite values.
Results may differ from a plain program's by a relative error of at most 0.0049.
Values may be sent and summed in bfloat16 or wider, within the bound.
A program may use at most 128 MiB of HBM per device.

v0:
```python
import jax
import jax.numpy as jnp
from jax import lax
from jax.sharding import PartitionSpec as P

BLK = 128


def level_norm(level_count, block_size, head_size):
    level_ids = jnp.arange(level_count, dtype=jnp.int32)
    doubling = jnp.exp2(jnp.maximum(level_ids - 1, 0).astype(jnp.float32))
    return lax.rsqrt(doubling * float(block_size * head_size))


def sibling(states, bit_index):
    block_count = states.shape[0]
    span = 2**bit_index
    grouped = states.reshape((block_count // span, span) + states.shape[1:]).sum(axis=1)
    paired = grouped.reshape((block_count // (2 * span), 2) + grouped.shape[1:])[:, ::-1]
    return jnp.repeat(paired.reshape(grouped.shape), span, axis=0)


def shards(grad_y, w_out, queries, keys, values, level_rows, level_table):
    token_count, width = queries.shape
    table_size, level_count, head_count = level_table.shape
    head_size = width // head_count
    block_count = token_count // BLK
    local_bits = block_count.bit_length() - 1
    device_bits = lax.axis_size("seq").bit_length() - 1
    position = lax.axis_index("seq")
    highest = lax.Precision.HIGHEST
    columns = w_out
    grad_sum = lax.dot_general(
        lax.all_gather(grad_y, "head", axis=1, tiled=True),
        columns,
        (((1,), (1,)), ((), ())),
        preferred_element_type=jnp.float32,
    )
    grad_out = grad_sum.astype(jnp.bfloat16)
    one_hot = (level_rows[:, None] == jnp.arange(table_size, dtype=jnp.int32)[None, :]).astype(
        jnp.float32
    )
    weights = jnp.dot(
        one_hot, level_table.reshape(table_size, level_count * head_count), precision=highest
    )
    weights = (
        weights.reshape(token_count, level_count, head_count)
        * level_norm(level_count, BLK, head_size)[None, :, None]
    )
    block_shape = (block_count, BLK, head_count, head_size)
    query_blocks = queries.reshape(block_shape)
    key_blocks = keys.reshape(block_shape)
    value_blocks = values.reshape(block_shape)
    grad_blocks = grad_out.reshape(block_shape)
    weight_blocks = weights.reshape(block_count, BLK, level_count, head_count)
    causal = (jnp.arange(BLK)[:, None] >= jnp.arange(BLK)[None, :]).astype(jnp.float32)
    intra_weight = jnp.transpose(weight_blocks[:, :, 0, :], (0, 2, 1))[:, :, :, None] * causal
    intra_grad = (
        jnp.einsum("bthp,bshp->bhts", grad_blocks, value_blocks, preferred_element_type=jnp.float32)
        * intra_weight
    ).astype(jnp.bfloat16)
    intra_score = (
        jnp.einsum("bthp,bshp->bhts", query_blocks, key_blocks, preferred_element_type=jnp.float32)
        * intra_weight
    ).astype(jnp.bfloat16)
    query_grad = jnp.einsum(
        "bhts,bshp->bthp", intra_grad, key_blocks, preferred_element_type=jnp.float32
    )
    key_grad = jnp.einsum(
        "bhts,bthp->bshp", intra_grad, query_blocks, preferred_element_type=jnp.float32
    )
    value_grad = jnp.einsum(
        "bhts,bthp->bshp", intra_score, grad_blocks, preferred_element_type=jnp.float32
    )
    states = jnp.einsum(
        "bthi,bthj->bhij", key_blocks, value_blocks, preferred_element_type=jnp.float32
    )
    block_ids = jnp.arange(block_count, dtype=jnp.int32)
    adjoint = jnp.zeros_like(states)
    for bit_index in range(local_bits):
        present = (block_ids >> bit_index & 1).astype(jnp.float32)[:, None, None, None]
        bucket = (sibling(states, bit_index) * present).astype(jnp.bfloat16)
        level_weight = weight_blocks[:, :, bit_index + 1, :][..., None]
        query_grad = query_grad + level_weight * jnp.einsum(
            "bthj,bhij->bthi", grad_blocks, bucket, preferred_element_type=jnp.float32
        )
        weighted = (level_weight * query_blocks).astype(jnp.bfloat16)
        adjoint_part = (
            jnp.einsum("bthi,bthj->bhij", weighted, grad_blocks, preferred_element_type=jnp.float32)
            * present
        )
        adjoint = adjoint + sibling(adjoint_part, bit_index)
    flat_query = queries.reshape(token_count, head_count, head_size)
    flat_grad = grad_out.reshape(token_count, head_count, head_size)
    device_total = states.sum(axis=0)
    device_flags = [
        (position >> bit_index & 1).astype(jnp.float32) for bit_index in range(device_bits)
    ]
    device_parts = []
    for bit_index in range(device_bits):
        level_weight = weights[:, local_bits + bit_index + 1, :][..., None]
        weighted = (level_weight * flat_query).astype(jnp.bfloat16)
        device_parts.append(
            jnp.einsum("thi,thj->hij", weighted, flat_grad, preferred_element_type=jnp.float32)
            * device_flags[bit_index]
        )

    def membership(row_count):
        peers = jnp.arange(row_count, dtype=jnp.int32)
        columns = []
        for bit_index in range(device_bits):
            inside = (
                (peers >> bit_index + 1 == position >> bit_index + 1)
                & (peers >> bit_index & 1 == 0)
                & (position >> bit_index & 1 == 1)
            )
            columns.append(inside.astype(jnp.float32))
        return jnp.stack(columns, axis=1)

    segment = lax.all_gather(device_total[None], "seq", axis=0, tiled=True)
    stacked = jnp.einsum("ne,nhij->ehij", membership(segment.shape[0]), segment, precision=highest)
    buckets = [stacked[bit_index] for bit_index in range(device_bits)]
    adjoint_stack = jnp.stack(device_parts, axis=0)
    carried = lax.psum_scatter(
        jnp.einsum(
            "ne,ehij->nhij", membership(lax.axis_size("seq") * 1), adjoint_stack, precision=highest
        ),
        "seq",
        scatter_dimension=0,
        tiled=True,
    )[0]
    for bit_index in range(device_bits):
        level_weight = weight_blocks[:, :, local_bits + bit_index + 1, :][..., None]
        query_grad = query_grad + level_weight * jnp.einsum(
            "bthj,hij->bthi",
            grad_blocks,
            buckets[bit_index].astype(jnp.bfloat16),
            preferred_element_type=jnp.float32,
        )
    adjoint_all = (adjoint + carried[None]).astype(jnp.bfloat16)
    key_grad = key_grad + jnp.einsum(
        "bshj,bhij->bshi", value_blocks, adjoint_all, preferred_element_type=jnp.float32
    )
    value_grad = value_grad + jnp.einsum(
        "bshi,bhij->bshj", key_blocks, adjoint_all, preferred_element_type=jnp.float32
    )
    return (
        query_grad.reshape(token_count, width),
        key_grad.reshape(token_count, width),
        value_grad.reshape(token_count, width),
    )


def solution(mesh):
    return jax.shard_map(
        shards,
        mesh=mesh,
        in_specs=(
            P("seq", "head"),
            P("head", None),
            P("seq", "head"),
            P("seq", "head"),
            P("seq", "head"),
            P("seq"),
            P(None, None, "head"),
        ),
        out_specs=(P("seq", "head"), P("seq", "head"), P("seq", "head")),
        check_vma=False,
    )
```

profile of v0, /device:TPU:2, one launch (start us, length us, event | category | flops | bytes accessed | tf_op | source)
XLA Modules:
  0.0 390.7 jit_solution(12083027111815541625)
XLA Ops:
  7.2 0.7 all-gather.4.cloned.1.call-update
  8.0 1.2 reshape.258
  9.1 1.4 reshape.261
  10.5 1.1 bitcast_reduce_fusion.1
  11.7 0.8 reduce_sum.28
  12.6 0.4 convolution_multiply_fusion.7
  13.0 1.3 copy.198
  14.4 32.1 %all-gather.4.cloned.1.call-done = bf16[512,4096]{1,0:T(8,128)(2,1)} async-done(((bf16[512,512]{1,0:T(8,128)(2,1)}), bf16[512,4096]{1,0:T(8,128)(2,1)}) %all-gather.4.cloned.1.call-update) | async-done | bytes 4194320 | tf_op jit(solution)/shard_map/all_gather | solution.py:34
  46.5 5.8 %convolution_convert_fusion = bf16[512,512]{0,1:T(8,128)(2,1)S(1)} fusion(bf16[512,4096]{1,0:T(8,128)(2,1)} %all-gather.4.cloned.1.call-done, bf16[512,4096]{1,0:T(8,128)(2,1)} %param.8), kind=kOutput, calls=%fused_computation.40 | convolution fusion | flops 2147745792 | bytes 8912896 | tf_op jit(solution)/shard_map/dot_general | solution.py:33
  52.3 0.3 fusion.35
  52.6 0.3 fusion.33
  52.9 0.3 fusion.31
  53.3 0.3 fusion.29
  53.6 0.3 fusion.27
  53.9 3.9 %fusion.2 = f32[32,4,128,128]{3,0,2,1:T(8,128)S(1)} fusion(f32[5,4,128,128]{3,2,1,0:T(8,128)S(1)} %fusion.27, pred[32,5]{0,1:T(8,128)(4,1)S(1)} %stack.17), kind=kOutput, calls=%fused_computation.2 | convolution fusion | flops 125829120 | bytes 9699488 | tf_op jit(solution)/shard_map/ne,ehij->nhij/dot_general | solution.py:125
  57.8 8.3 %copy.168 = f32[32,4,128,128]{3,2,1,0:T(8,128)} copy(f32[32,4,128,128]{3,0,2,1:T(8,128)S(1)} %fusion.2) | data formatting | bytes 16777216 | tf_op jit(solution)/shard_map/ne,ehij->nhij/dot_general | solution.py:125
  66.2 1.0 copy-done.8
  67.3 1.1 rev.8
  68.4 0.8 reverse.6
  69.3 2.0 fusion.39
  71.7 0.8 bitcast_reduce_fusion
  72.5 1.0 convolution_multiply_fusion.1
  73.5 1.1 reverse_add_fusion
  74.6 2.5 copy.156
  77.2 0.6 fusion.23
  77.7 1.3 convolution_bitcast_fusion.1
  79.1 1.3 convolution_bitcast_fusion.9
  80.3 1.7 fusion.25
  82.0 1.9 fusion.22
  83.9 1.6 fusion.20
  85.4 63.2 %all-gather.6.cloned.1.call-done = f32[128,128,128]{2,1,0:T(8,128)} async-done(((f32[4,128,128]{2,1,0:T(8,128)}), f32[128,128,128]{2,1,0:T(8,128)}) %all-gather.6.cloned.1.call-update) | async-done | bytes 8388624 | tf_op jit(solution)/shard_map/all_gather | solution.py:120
  148.6 10.5 %fusion.4 = bf16[5,4,128,128]{3,0,2,1:T(8,128)(2,1)S(1)} fusion(f32[32,4,128,128]{3,2,1,0:T(8,128)} %bitcast.212, pred[32,5]{0,1:T(8,128)(4,1)S(1)} %stack.17), kind=kOutput, calls=%fused_computation.6 | convolution fusion | flops 126156800 | bytes 9044128 | tf_op jit(solution)/shard_map/ne,nhij->ehij/dot_general | solution.py:121
  159.1 1.0 fusion.96
  160.4 0.6 fusion.18
  161.0 0.7 fusion.16
  161.7 0.7 fusion.14
  162.3 0.7 fusion.12
  163.0 0.7 fusion.10
  163.7 0.7 copy.148
  164.3 1.0 copy.312
  165.4 213.6 %reduce-scatter.2.cloned.1.call-done = f32[1,4,128,128]{3,2,1,0:T(8,128)} async-done(((f32[32,4,128,128]{3,2,1,0:T(8,128)}), f32[1,4,128,128]{3,2,1,0:T(8,128)}) %reduce-scatter.2.cloned.1.call-update) | async-done | bytes 262160 | tf_op jit(solution)/shard_map/reduce_scatter | solution.py:124
  378.9 1.1 copy.169
  380.2 0.3 fusion.7
  380.5 0.7 copy.173
  381.2 1.0 copy.311
  382.2 0.5 fusion.8
  382.7 0.4 copy.178
  383.1 1.0 copy.310
  (57 shorter events, 1.3 us)
Async XLA Ops:
  7.2 5.4 %copy-start = (f32[128,12,4]{0,2,1:T(4,128)S(1)}, f32[128,12,4]{0,2,1:T(4,128)}, u32[]{:S(2)}) copy-start(f32[128,12,4]{0,2,1:T(4,128)} %param.13) | copy-start | bytes 73732
  7.2 39.3 %all-gather.4.cloned.1.call-start = ((), (), s32[]{:S(2)}) async-start(), calls=%async_computation.1 | async-start | bytes 4718592 | tf_op jit(solution)/shard_map/all_gather | solution.py:34
  7.9 140.7 %all-gather.6.cloned.1.call-start = ((), (), s32[]{:S(2)}) async-start(), calls=%async_computation.3 | async-start | bytes 8650752 | tf_op jit(solution)/shard_map/all_gather | solution.py:120
  9.1 3.3 copy-start.2
  10.5 2.1 copy-start.12
  12.5 366.5 %reduce-scatter.2.cloned.1.call-start = ((), (), s32[]{:S(2)}) async-start(), calls=%async_computation.2 | async-start | bytes 8650752 | tf_op jit(solution)/shard_map/reduce_scatter | solution.py:124
  66.1 1.0 copy-start.8
  67.3 1.1 copy-start.9
  68.4 2.9 copy-start.7
  73.5 3.6 copy-start.3
  82.0 1.9 copy-start.10
  159.1 1.2 copy-start.5
  163.6 216.4 %copy-start.6 = (f32[2,2,4,128,128]{3,4,2,1,0:T(8,128)S(1)}, f32[2,2,4,128,128]{3,4,2,1,0:T(8,128)}, u32[]{:S(2)}) copy-start(f32[2,2,4,128,128]{3,4,2,1,0:T(8,128)} %copy.156) | copy-start | bytes 3145732
  164.3 215.8 %copy-start.4 = (f32[4,128,4,128]{3,1,2,0:T(8,128)S(1)}, f32[4,128,4,128]{3,1,2,0:T(8,128)}, u32[]{:S(2)}) copy-start(f32[4,128,4,128]{3,1,2,0:T(8,128)} %convolution_bitcast_fusion.1) | copy-start | bytes 3145732
  380.5 1.7 copy-start.11
  382.2 1.9 copy-start.1
Sparse Core Ops, SparseCore 0:
  9.9 36.5 all-gather.3
  49.1 99.5 all-gather.5
  152.7 226.2 reduce-scatter.1
where the time goes:
time: 391 us
  waiting for transfers between devices  310 us (79%)
  matrix products  37.4 us (10%)
  local copies, waits for them, and re-layouts  25.1 us (6%)
  between operations  14.2 us (4%)
  other arithmetic  4.28 us (1%)
    reduce_scatter x1, waiting for transfers between devices, shards(): lax.psum_scatter(jnp.einsum('ne,ehij->nhij', membership(lax.axis_size('se...  214 us
    all_gather x1, waiting for transfers between devices, shards(): segment = lax.all_gather(device_total[None], 'seq', axis=0, tiled=True)  63.2 us
    all_gather x1, waiting for transfers between devices, shards(): lax.all_gather(grad_y, 'head', axis=1, tiled=True)  32.1 us
    dot_general x1, matrix products, shards(): jnp.einsum('ne,nhij->ehij', membership(segment.shape[0]), segment, precis...  10.5 us
    dot_general x1, local copies, waits for them, and re-layouts, shards(): jnp.einsum('ne,ehij->nhij', membership(lax.axis_size('seq') * 1), adjoint...  8.28 us
  transfers between devices with their start and end apart: 3, of which 3 were waited for; matrix products, arithmetic and copies ran while one was open for 15% of the time, Pallas kernels for 0%

commit v1 on v0

--- a/solution.py
+++ b/solution.py
@@ -4,6 +4,27 @@
 from jax.sharding import PartitionSpec as P
 
 BLK = 128
+
+
+def gather_around(x, axis, dim):
+    size, index, span = (lax.axis_size(axis), lax.axis_index(axis), x.shape[dim])
+    right = [(i, (i + 1) % size) for i in range(size)]
+    backward = [(i, (i - 1) % size) for i in range(size)]
+    result = jnp.zeros((*x.shape[:dim], size * span, *x.shape[dim + 1 :]), x.dtype)
+    result = lax.dynamic_update_slice_in_dim(result, x, index * span, axis=dim)
+    from_left = from_right = x
+    half = size // 2
+    for step in range(1, half + 1):
+        from_left = lax.ppermute(from_left, axis, right)
+        result = lax.dynamic_update_slice_in_dim(
+            result, from_left, (index - step) % size * span, axis=dim
+        )
+        if step < size - half:
+            from_right = lax.ppermute(from_right, axis, backward)
+            result = lax.dynamic_update_slice_in_dim(
+                result, from_right, (index + step) % size * span, axis=dim
+            )
+    return result
 
 
 def level_norm(level_count, block_size, head_size):
@@ -31,7 +52,7 @@
     highest = lax.Precision.HIGHEST
     columns = w_out
     grad_sum = lax.dot_general(
-        lax.all_gather(grad_y, "head", axis=1, tiled=True),
+        gather_around(grad_y, "head", 1),
         columns,
         (((1,), (1,)), ((), ())),
         preferred_element_type=jnp.float32,

time: 391 us -> 363 us (0.928)
  waiting for transfers between devices: 310 us -> 263 us
  local copies, waits for them, and re-layouts: 25.1 us -> 36 us
  starting transfers between devices: 0.12 us -> 5.45 us
    all_gather x1, waiting for transfers between devices: 63.2 us -> 28.4 us  [shards(): segment = lax.all_gather(device_total[None], 'seq', axis=0, tiled=True)]
    all_gather x1 -> x0, waiting for transfers between devices: 32.1 us -> none  [shards(): lax.all_gather(grad_y, 'head', axis=1, tiled=True)]
    ppermute x0 -> x7, waiting for transfers between devices: none -> 21.2 us  [the longest x4 21.2 us: gather_around(): from_left = lax.ppermute(from_left, axis, right)]
    dynamic_update_slice x0 -> x8, local copies, waits for them, and re-layouts: none -> 5.89 us  [the longest x4 2.35 us: gather_around(): lax.dynamic_update_slice_in_dim(result, from_left, (index - step) % size...]
    ppermute x0 -> x7, starting transfers between devices: none -> 5.37 us  [the longest x3 5.35 us: gather_around(): from_right = lax.ppermute(from_right, axis, backward)]
  transfers between devices with their start and end apart: 3 -> 9, of which waited for: 3 -> 6; matrix products, arithmetic and copies ran while one was open for 15% -> 17% of each run, Pallas kernels for 0% -> 0%
where the time goes in v1:
time: 363 us; the launch traced here: 362 us
  waiting for transfers between devices  263 us (72%)
  matrix products  37.2 us (10%)
  local copies, waits for them, and re-layouts  36 us (10%)
  between operations  14.8 us (4%)
  other arithmetic  5.74 us (2%)
  starting transfers between devices  5.45 us (2%)
    reduce_scatter x1, waiting for transfers between devices, shards(): lax.psum_scatter(jnp.einsum('ne,ehij->nhij', membership(lax.axis_size('se...  213 us
    all_gather x1, waiting for transfers between devices, shards(): segment = lax.all_gather(device_total[None], 'seq', axis=0, tiled=True)  28.4 us
    ppermute x4, waiting for transfers between devices, gather_around(): from_left = lax.ppermute(from_left, axis, right)  21.2 us
    dot_general x1, matrix products, shards(): jnp.einsum('ne,nhij->ehij', membership(segment.shape[0]), segment, precis...  10.6 us
    dot_general x1, local copies, waits for them, and re-layouts, shards(): jnp.einsum('ne,ehij->nhij', membership(lax.axis_size('seq') * 1), adjoint...  8.26 us
  transfers between devices with their start and end apart: 9, of which 6 were waited for; matrix products, arithmetic and copies ran while one was open for 17% of the time, Pallas kernels for 0%

profile of v1, /device:TPU:2, one launch (start us, length us, event | category | flops | bytes accessed | tf_op | source)
XLA Modules:
  0.0 362.0 jit_solution(10948709033159824583)
XLA Ops:
  7.2 1.2 reshape.261
  8.5 1.2 reshape.258
  9.7 1.1 bitcast_reduce_fusion.1
  10.8 0.8 reduce_sum.28
  11.7 1.7 collective-permute-start.1
  13.8 6.4 %collective-permute-done = bf16[512,512]{1,0:T(8,128)(2,1)S(1)} collective-permute-done((bf16[512,512]{1,0:T(8,128)(2,1)S(1)}, bf16[512,512]{1,0:T(8,128)(2,1)S(1)}, u32[]{:S(2)}, u32[]{:S(2)}) %collective-permute-start) | collective-permute-done | bytes 524320 | tf_op jit(solution)/shard_map/ppermute | solution.py:18
  20.3 2.0 collective-permute-start.3
  22.3 6.7 %collective-permute-done.2 = bf16[512,512]{1,0:T(8,128)(2,1)} collective-permute-done((bf16[512,512]{1,0:T(8,128)(2,1)S(1)}, bf16[512,512]{1,0:T(8,128)(2,1)}, u32[]{:S(2)}, u32[]{:S(2)}) %collective-permute-start.2) | collective-permute-done | bytes 524320 | tf_op jit(solution)/shard_map/ppermute | solution.py:18
  29.2 1.3 copy.198
  31.1 1.3 constant_dynamic-update-slice_fusion.7
  32.4 1.6 collective-permute-start.5
  34.1 3.8 %collective-permute-done.4 = bf16[512,512]{1,0:T(8,128)(2,1)} collective-permute-done((bf16[512,512]{1,0:T(8,128)(2,1)}, bf16[512,512]{1,0:T(8,128)(2,1)}, u32[]{:S(2)}, u32[]{:S(2)}) %collective-permute-start.4) | collective-permute-done | bytes 524320 | tf_op jit(solution)/shard_map/ppermute | solution.py:18
  37.9 1.1 constant_dynamic-update-slice_fusion.5
  39.0 1.1 constant_dynamic-update-slice_fusion.4
  40.2 1.1 constant_dynamic-update-slice_fusion.3
  41.3 1.1 constant_dynamic-update-slice_fusion.2
  42.5 4.3 %collective-permute-done.6 = bf16[512,512]{1,0:T(8,128)(2,1)S(1)} collective-permute-done((bf16[512,512]{1,0:T(8,128)(2,1)}, bf16[512,512]{1,0:T(8,128)(2,1)S(1)}, u32[]{:S(2)}, u32[]{:S(2)}) %collective-permute-start.6) | collective-permute-done | bytes 524320 | tf_op jit(solution)/shard_map/ppermute | solution.py:18
  46.8 2.4 convolution_convert_fusion
  50.8 3.9 %fusion.2 = f32[32,4,128,128]{3,0,2,1:T(8,128)S(1)} fusion(f32[5,4,128,128]{3,2,1,0:T(8,128)S(1)} %fusion.27, pred[32,5]{0,1:T(8,128)(4,1)S(1)} %stack.17), kind=kOutput, calls=%fused_computation.2 | convolution fusion | flops 125829120 | bytes 9699488 | tf_op jit(solution)/shard_map/ne,ehij->nhij/dot_general | solution.py:146
  54.7 8.3 %copy.168 = f32[32,4,128,128]{3,2,1,0:T(8,128)} copy(f32[32,4,128,128]{3,0,2,1:T(8,128)S(1)} %fusion.2) | data formatting | bytes 16777216 | tf_op jit(solution)/shard_map/ne,ehij->nhij/dot_general | solution.py:146
  63.0 1.0 copy-done.6
  64.2 1.1 rev.8
  65.2 1.2 reverse.6
  66.5 1.0 fusion.39
  67.5 1.4 fusion.40
  69.1 1.6 bitcast_reduce_fusion
  70.6 1.1 reverse.7
  71.8 1.0 convolution_multiply_fusion.1
  72.8 1.1 reverse_add_fusion
  73.9 2.6 copy.156
  77.0 1.3 convolution_bitcast_fusion.1
  78.4 1.3 convolution_bitcast_fusion.9
  79.6 1.6 fusion.25
  81.3 1.8 fusion.22
  83.1 1.6 fusion.20
  84.7 28.4 %all-gather.3.cloned.1.call-done = f32[128,128,128]{2,1,0:T(8,128)} async-done(((f32[4,128,128]{2,1,0:T(8,128)}), f32[128,128,128]{2,1,0:T(8,128)}) %all-gather.3.cloned.1.call-update) | async-done | bytes 8388624 | tf_op jit(solution)/shard_map/all_gather | solution.py:141
  113.1 10.6 %fusion.4 = bf16[5,4,128,128]{3,0,2,1:T(8,128)(2,1)S(1)} fusion(f32[32,4,128,128]{3,2,1,0:T(8,128)} %bitcast.212, pred[32,5]{0,1:T(8,128)(4,1)S(1)} %stack.17), kind=kOutput, calls=%fused_computation.6 | convolution fusion | flops 126156800 | bytes 9044128 | tf_op jit(solution)/shard_map/ne,nhij->ehij/dot_general | solution.py:142
  123.7 1.0 fusion.96
  124.6 0.9 fusion.18
  128.2 0.7 copy.148
  128.9 1.0 copy.312
  129.9 213.1 %reduce-scatter.2.cloned.1.call-done = f32[1,4,128,128]{3,2,1,0:T(8,128)} async-done(((f32[32,4,128,128]{3,2,1,0:T(8,128)}), f32[1,4,128,128]{3,2,1,0:T(8,128)}) %reduce-scatter.2.cloned.1.call-update) | async-done | bytes 262160 | tf_op jit(solution)/shard_map/reduce_scatter | solution.py:145
  343.0 1.1 copy.169
  344.1 1.4 fusion.38
  345.6 2.7 fusion.8
  348.3 2.6 copy.178
  350.8 2.3 copy.310
  354.1 1.0 copy.311
  (77 shorter events, 7.4 us)
Async XLA Ops:
  7.2 6.3 %copy-start = (f32[128,12,4]{0,2,1:T(4,128)S(1)}, f32[128,12,4]{0,2,1:T(4,128)}, u32[]{:S(2)}) copy-start(f32[128,12,4]{0,2,1:T(4,128)} %param.13) | copy-start | bytes 73732
  7.2 4.5 %copy-start.8 = (bf16[512,512]{1,0:T(8,128)(2,1)S(1)}, bf16[512,512]{1,0:T(8,128)(2,1)}, u32[]{:S(2)}) copy-start(bf16[512,512]{1,0:T(8,128)(2,1)} %param.7) | copy-start | bytes 1572868
  7.2 6.2 %copy-start.11 = (s32[512]{0:T(512)S(1)}, s32[512]{0:T(512)}, u32[]{:S(2)}) copy-start(s32[512]{0:T(512)} %param.12) | copy-start | bytes 6148
  7.2 105.9 %all-gather.3.cloned.1.call-start = ((), (), s32[]{:S(2)}) async-start(), calls=%async_computation.2 | async-start | bytes 8650752 | tf_op jit(solution)/shard_map/all_gather | solution.py:141
  9.6 19.5 %copy-start.2 = (bf16[4,128,4,128]{3,2,1,0:T(4,128)(2,1)}, bf16[4,128,4,128]{3,2,1,0:T(4,128)(2,1)S(1)}, u32[]{:S(2)}) copy-start(bf16[4,128,4,128]{3,2,1,0:T(4,128)(2,1)S(1)} %reshape.258) | copy-start | bytes 1572868
  11.6 331.4 %reduce-scatter.2.cloned.1.call-start = ((), (), s32[]{:S(2)}) async-start(), calls=%async_computation.1 | async-start | bytes 8650752 | tf_op jit(solution)/shard_map/reduce_scatter | solution.py:145
  11.7 8.6 %collective-permute-start = (bf16[512,512]{1,0:T(8,128)(2,1)S(1)}, bf16[512,512]{1,0:T(8,128)(2,1)S(1)}, u32[]{:S(2)}, u32[]{:S(2)}) collective-permute-start(bf16[512,512]{1,0:T(8,128)(2,1)S(1)} %copy-done.8), channel_id=1, source_target_pairs={{0,1},{1,2},{2,3},{3,4},{4,5},{5,6},{6,7},{7,0},{8,9},{9,10},{10,1... | collective-permute-start | bytes 1572872 | tf_op jit(solution)/shard_map/ppermute | solution.py:18
  11.7 8.7 %collective-permute-start.1 = (bf16[512,512]{1,0:T(8,128)(2,1)S(1)}, bf16[512,512]{1,0:T(8,128)(2,1)}, u32[]{:S(2)}, u32[]{:S(2)}) collective-permute-start(bf16[512,512]{1,0:T(8,128)(2,1)S(1)} %copy-done.8), channel_id=1, source_target_pairs={{0,7},{1,0},{2,1},{3,2},{4,3},{5,4},{6,5},{7,6},{8,15},{9,8},{10,9... | collective-permute-start | bytes 1572872 | tf_op jit(solution)/shard_map/ppermute | solution.py:23
  20.3 8.9 %copy-start.9 = (bf16[512,512]{1,0:T(8,128)(2,1)}, bf16[512,512]{1,0:T(8,128)(2,1)S(1)}, u32[]{:S(2)}) copy-start(bf16[512,512]{1,0:T(8,128)(2,1)S(1)} %collective-permute-done) | copy-start | bytes 1572868
  20.3 8.7 %collective-permute-start.2 = (bf16[512,512]{1,0:T(8,128)(2,1)S(1)}, bf16[512,512]{1,0:T(8,128)(2,1)}, u32[]{:S(2)}, u32[]{:S(2)}) collective-permute-start(bf16[512,512]{1,0:T(8,128)(2,1)S(1)} %collective-permute-done), channel_id=1, source_target_pairs={{0,1},{1,2},{2,3},{3,4},{4,5},{5,6},{6,7},{7,0},{8,9},{9,10},{10,1... | collective-permute-start | bytes 1572872 | tf_op jit(solution)/shard_map/ppermute | solution.py:18
  20.3 12.0 %collective-permute-start.3 = (bf16[512,512]{1,0:T(8,128)(2,1)}, bf16[512,512]{1,0:T(8,128)(2,1)}, u32[]{:S(2)}, u32[]{:S(2)}) collective-permute-start(bf16[512,512]{1,0:T(8,128)(2,1)} %collective-permute-done.1), channel_id=1, source_target_pairs={{0,7},{1,0},{2,1},{3,2},{4,3},{5,4},{6,5},{7,6},{8,15},{9,8},{10,9... | collective-permute-start | bytes 1572872 | tf_op jit(solution)/shard_map/ppermute | solution.py:23
  29.0 8.9 %collective-permute-start.4 = (bf16[512,512]{1,0:T(8,128)(2,1)}, bf16[512,512]{1,0:T(8,128)(2,1)}, u32[]{:S(2)}, u32[]{:S(2)}) collective-permute-start(bf16[512,512]{1,0:T(8,128)(2,1)} %collective-permute-done.2), channel_id=1, source_target_pairs={{0,1},{1,2},{2,3},{3,4},{4,5},{5,6},{6,7},{7,0},{8,9},{9,10},{10,1... | collective-permute-start | bytes 1572872 | tf_op jit(solution)/shard_map/ppermute | solution.py:18
  29.2 4.9 %copy-start.10 = (bf16[512,512]{1,0:T(8,128)(2,1)S(1)}, bf16[512,512]{1,0:T(8,128)(2,1)}, u32[]{:S(2)}) copy-start(bf16[512,512]{1,0:T(8,128)(2,1)} %copy-done.9) | copy-start | bytes 1572868
  31.1 15.7 %copy-start.12 = (bf16[512,4096]{1,0:T(8,128)(2,1)S(1)}, bf16[512,4096]{1,0:T(8,128)(2,1)}, u32[]{:S(2)}) copy-start(bf16[512,4096]{1,0:T(8,128)(2,1)} %param.8) | copy-start | bytes 12582916
  32.4 10.0 %collective-permute-start.5 = (bf16[512,512]{1,0:T(8,128)(2,1)}, bf16[512,512]{1,0:T(8,128)(2,1)S(1)}, u32[]{:S(2)}, u32[]{:S(2)}) collective-permute-start(bf16[512,512]{1,0:T(8,128)(2,1)} %collective-permute-done.3), channel_id=1, source_target_pairs={{0,7},{1,0},{2,1},{3,2},{4,3},{5,4},{6,5},{7,6},{8,15},{9,8},{10,9... | collective-permute-start | bytes 1572872 | tf_op jit(solution)/shard_map/ppermute | solution.py:23
  37.9 8.8 %collective-permute-start.6 = (bf16[512,512]{1,0:T(8,128)(2,1)}, bf16[512,512]{1,0:T(8,128)(2,1)S(1)}, u32[]{:S(2)}, u32[]{:S(2)}) collective-permute-start(bf16[512,512]{1,0:T(8,128)(2,1)} %collective-permute-done.4), channel_id=1, source_target_pairs={{0,1},{1,2},{2,3},{3,4},{4,5},{5,6},{6,7},{7,0},{8,9},{9,10},{10,1... | collective-permute-start | bytes 1572872 | tf_op jit(solution)/shard_map/ppermute | solution.py:18
  62.9 1.0 copy-start.6
  70.6 5.8 %copy-start.3 = (bf16[4,128,4,128]{3,2,1,0:T(4,128)(2,1)S(1)}, bf16[4,128,4,128]{3,2,1,0:T(4,128)(2,1)}, u32[]{:S(2)}) copy-start(bf16[4,128,4,128]{3,2,1,0:T(4,128)(2,1)} %copy-done.2) | copy-start | bytes 1572868
  78.3 4.7 %copy-start.7 = (bf16[4,4,128,128]{3,2,1,0:T(8,128)(2,1)S(1)}, bf16[4,4,128,128]{3,2,1,0:T(8,128)(2,1)}, u32[]{:S(2)}) copy-start(bf16[4,4,128,128]{3,2,1,0:T(8,128)(2,1)} %fusion.39) | copy-start | bytes 1572868
  113.1 11.5 %copy-start.5 = (f32[4,128,4,128]{3,1,2,0:T(8,128)S(1)}, f32[4,128,4,128]{3,1,2,0:T(8,128)}, u32[]{:S(2)}) copy-start(f32[4,128,4,128]{3,1,2,0:T(8,128)} %fusion.20) | copy-start | bytes 3145732
  344.1 9.0 %copy-start.4 = (f32[4,128,4,128]{3,1,2,0:T(8,128)S(1)}, f32[4,128,4,128]{3,1,2,0:T(8,128)}, u32[]{:S(2)}) copy-start(f32[4,128,4,128]{3,1,2,0:T(8,128)} %convolution_bitcast_fusion.1) | copy-start | bytes 3145732
  350.8 4.3 %copy-start.1 = (f32[128,12,4]{0,2,1:T(4,128)S(1)}, f32[128,12,4]{0,2,1:T(4,128)}, u32[]{:S(2)}) copy-start(f32[128,12,4]{0,2,1:T(4,128)} %param.13) | copy-start | bytes 73732
Sparse Core Ops, SparseCore 0:
  11.7 101.3 all-gather.2
  117.1 225.8 reduce-scatter.1
